TPU v7x, 32 devices: a whole 2x2x4 slice. The times are simulated.
32 devices in a mesh: img: 8 (over z, y), row: 4 (over x, core).
Axes of the slice: x: 2, y: 2, z: 4, core: 2. Of those that a mesh axis runs over, the one named last changes fastest.
Arguments:
- images: bfloat16 [24, 32, 32, 384], P('img', 'row'), may hold values from -8 to 8
- level_count: int32 [24], P('img'), may hold values from 2 to 1280
- level_index: int32 [24], P('img'), may hold values from 0 to 1278, as said below
- labels: int32 [24], P('img'), may hold values from 0 to 999
- first_gain: bfloat16 [384], replicated, may hold values from 0.5 to 1.5
- first_shift: bfloat16 [384], replicated, may hold values from -1.75 to 1.75
- first_kernel: bfloat16 [3456, 384], replicated, may hold values from -0.109375 to 0.109375
- first_offset: bfloat16 [384], replicated, may hold values from -1.75 to 1.75
- embed_weight: bfloat16 [768, 768], replicated, may hold values from -0.21875 to 0.21875
- embed_offset: bfloat16 [768], replicated, may hold values from -1.75 to 1.75
- class_table: bfloat16 [1000, 768], replicated, may hold values from -6 to 6
- second_gain: bfloat16 [384], replicated, may hold values from 0.5 to 1.5
- second_shift: bfloat16 [384], replicated, may hold values from -1.75 to 1.75
- second_kernel: bfloat16 [3456, 384], replicated, may hold values from -0.109375 to 0.109375
- second_offset: bfloat16 [384], replicated, may hold values from -1.75 to 1.75
- third_gain: bfloat16 [384], replicated, may hold values from 0.5 to 1.5
- third_shift: bfloat16 [384], replicated, may hold values from -1.75 to 1.75
- joint_weight: bfloat16 [384, 1152], replicated, may hold values from -0.3125 to 0.3125
- joint_offset: bfloat16 [768], replicated, may hold values from -1.75 to 1.75
- output_weight: bfloat16 [384, 384], replicated, may hold values from -2.5 to 2.5
- output_offset: bfloat16 [384], replicated, may hold values from -1.75 to 1.75
- cotangent: bfloat16 [24, 32, 32, 384], P('img', 'row'), may hold values from -8 to 8
Outputs:
- result: bfloat16 [24, 32, 32, 384], P('img', 'row')
- images_gradient: float32 [24, 32, 32, 384], P('img', 'row')
- first_gain_gradient: float32 [384], P('row')
- first_shift_gradient: float32 [384], P('row')
- first_kernel_gradient: float32 [3456, 384], P('row')
- first_offset_gradient: float32 [384], P('row')
- embed_weight_gradient: float32 [768, 768], P('row')
- embed_offset_gradient: float32 [768], P('row')
- class_table_gradient: float32 [1000, 768], P('row')
- second_gain_gradient: float32 [384], P('row')
- second_shift_gradient: float32 [384], P('row')
- second_kernel_gradient: float32 [3456, 384], P('row')
- second_offset_gradient: float32 [384], P('row')
- third_gain_gradient: float32 [384], P('row')
- third_shift_gradient: float32 [384], P('row')
- joint_weight_gradient: float32 [384, 1152], P('row')
- joint_offset_gradient: float32 [768], P('row')
- output_weight_gradient: float32 [384, 384], P('row')
- output_offset_gradient: float32 [384], P('row')
Inputs may be any that keep to these rules, and one draw needn't show every extreme that they name: Each image's level_index is below its level_count - 1.
All inputs are finite; a program needn't handle non-finite values.
Results may differ from a plain program's by a relative error of at most 0.017.
Values may be sent and summed in bfloat16 or wider, within the bound.
A program may use at most 192 MiB of HBM per device.

v0:
```python
import math

import jax
import jax.numpy as jnp
from jax import lax
from jax.experimental import pallas as pl
from jax.experimental.pallas import tpu as pltpu
from jax.sharding import PartitionSpec as P

GROUPS = 32
HEAD = 64
EMB = 768
MESH = pl.DeviceIdType.MESH

norm_eps = 1e-05
sigma_least = 0.002
sigma_most = 80.0
sigma_power = 7.0
highest = lax.Precision.HIGHEST
float_type = jnp.float32
low_type = jnp.bfloat16
contract_rows = (((0,), (0,)), ((), ()))
contract_cols = (((1,), (1,)), ((), ()))


def noise_features(level_count, level_index):
    position = (level_index.astype(jnp.float32) + 1.0) / (level_count.astype(jnp.float32) - 1.0)
    low_root = sigma_least ** (1.0 / sigma_power)
    high_root = sigma_most ** (1.0 / sigma_power)
    noise_level = (low_root + position * (high_root - low_root)) ** sigma_power
    noise_time = 250.0 * jnp.log(noise_level)
    half_width = EMB // 2
    frequency = jnp.exp(-math.log(10000.0) * jnp.arange(half_width, dtype=jnp.float32) / half_width)
    angles = noise_time[:, None] * frequency[None, :]
    return jnp.concatenate([jnp.cos(angles), jnp.sin(angles)], axis=-1)


def silu_slope(values):
    sigmoid_part = jax.nn.sigmoid(values)
    return sigmoid_part * (1.0 + values * (1.0 - sigmoid_part))


def normalize(values, centre, scaled):
    return (values - centre) * scaled


def group_fold(v):
    return v.reshape(v.shape[:-1] + (GROUPS, v.shape[-1] // GROUPS))


def group_back(upstream, normed, scaled):
    image_count, pixels, channels = upstream.shape
    first_sum = jnp.sum(group_fold(jnp.sum(upstream, axis=1)), axis=-1)
    second_sum = jnp.sum(group_fold(jnp.sum(upstream * normed, axis=1)), axis=-1)
    first_sum, second_sum = lax.psum((first_sum, second_sum), "row")
    entries = pixels * lax.axis_size("row") * (channels // GROUPS)
    per = channels // GROUPS
    first_sum = jnp.repeat(first_sum / entries, per, axis=-1)
    second_sum = jnp.repeat(second_sum / entries, per, axis=-1)
    return scaled * (upstream - first_sum[:, None, :] - normed * second_sum[:, None, :])


def padded_grads(activity):
    size, length = lax.axis_size("row"), activity.shape[1]
    up = [(i, i + 1) for i in range(size - 1)]
    down = [(j, i) for i, j in up]
    last = lax.slice_in_dim(activity, length - 1, length, axis=1)
    initial = lax.slice_in_dim(activity, 0, 1, axis=1)
    before = lax.ppermute(last, "row", up)
    after = lax.ppermute(initial, "row", down)
    framed = jnp.concatenate([before, activity, after], axis=1)
    return jnp.pad(framed, ((0, 0), (0, 0), (1, 1), (0, 0)))


def backward_patches(framed, stripe_rows, image_width):
    pieces = [
        framed[
            :, 2 - row_tap : 2 - row_tap + stripe_rows, 2 - col_tap : 2 - col_tap + image_width, :
        ]
        for row_tap in range(3)
        for col_tap in range(3)
    ]
    joined = jnp.concatenate(pieces, axis=-1)
    return joined.reshape(-1, joined.shape[-1])


def transpose_product(columns, kernel):
    channels = kernel.shape[1]
    stacked = columns.reshape(columns.shape[0], 9, channels)
    kernel_taps = kernel.reshape(9, kernel.shape[0] // 9, channels)
    return lax.dot_general(
        stacked, kernel_taps, (((1, 2), (0, 2)), ((), ())), preferred_element_type=float_type
    )


def peers():
    i = lax.axis_index("img")
    r = lax.axis_index("row")
    c = lax.rem(r, 2)
    near = r + 1 - 2 * c
    return (i, r, c, {1: (i, near), 2: (i, lax.rem(r + 2, 4)), 3: (i, 3 - r)})


def half_silu(v):
    h = 0.5 * v
    return h * jnp.tanh(h) + h


def col_iota(n, width, channels):
    return lax.rem(lax.broadcasted_iota(jnp.int32, (n, channels), 0), width)


def fill_row(buf, start, act, channels, width):
    col = lax.broadcasted_iota(jnp.int32, (width, channels), 0)
    left = jnp.where(col == 0, 0.0, pltpu.roll(act, 1, 0))
    right = jnp.where(col == width - 1, 0.0, pltpu.roll(act, width - 1, 0))
    rows = pl.ds(start, width)
    buf[rows, 0:channels] = left.astype(low_type)
    buf[rows, channels : 2 * channels] = act.astype(low_type)
    buf[rows, 2 * channels : 3 * channels] = right.astype(low_type)


def pack_stats(first, second):
    channels = first.shape[1]
    row = lax.broadcasted_iota(jnp.int32, (8, channels), 0)

    def terms(v):
        a = v.astype(low_type).astype(float_type)
        b = (v - a).astype(low_type).astype(float_type)
        c = v - a - b
        return jnp.where(row == 0, a, jnp.where(row == 1, b, jnp.where(row == 2, c, 0.0)))

    return jnp.concatenate([terms(first), terms(second)], axis=0).astype(low_type)


def block_ones(channels, per):
    a = lax.broadcasted_iota(jnp.int32, (channels, channels), 0)
    b = lax.broadcasted_iota(jnp.int32, (channels, channels), 1)
    a = lax.shift_right_logical(a * 43691, 19)
    b = lax.shift_right_logical(b * 43691, 19)
    return jnp.where(a == b, 1.0, 0.0).astype(low_type)


def combine_stats(parts, ones, entries):
    total = jnp.dot(jnp.concatenate(parts, axis=0), ones, preferred_element_type=float_type)
    first = total[0:8] + total[16:24] + total[32:40] + total[48:56]
    second = total[8:16] + total[24:32] + total[40:48] + total[56:64]
    first = jnp.sum(first, axis=0, keepdims=True) * (1.0 / entries)
    second = jnp.sum(second, axis=0, keepdims=True) * (1.0 / entries)
    return first, second


def forward_kernel(
    x_ref, vec_ref, mod_ref, w1_any, w2_any,
    hid_ref, mid_ref, att_ref, act1_ref, act2_ref, st_ref,
    w1, w2, ones, abuf, m1, m3, got, wsem, ssem, rsem,
):
    images, pixels, channels = x_ref.shape
    width = 32
    edge = pixels - width
    entries = 4.0 * pixels * (channels // GROUPS)
    i, r, c, who = peers()
    load1 = pltpu.make_async_copy(w1_any, w1, wsem.at[0])
    load2 = pltpu.make_async_copy(w2_any, w2, wsem.at[1])
    load1.start()
    load2.start()
    barrier = pltpu.get_barrier_semaphore()
    for k in (1, 2, 3):
        pl.semaphore_signal(barrier, inc=1, device_id=who[k], device_id_type=MESH)
    ones[...] = block_ones(channels, channels // GROUPS)
    inner = pl.multiple_of(edge * (1 - c), width)
    outer = pl.multiple_of(edge * c, width)
    inner_live = None
    outer_live = jnp.logical_and(r > 0, r < 3)
    stat = pl.ds(0, 16)
    halo = pl.ds(16, width)

    def copies(p, b):
        full = p < 2
        rows = pl.ds(0, 48) if full else stat
        return [
            pltpu.make_async_remote_copy(
                src.at[p, b, rs], got.at[p, b, k - 1, rs], ssem.at[p, b, k - 1],
                rsem.at[p, b, k - 1], device_id=who[k], device_id_type=MESH,
            )
            for k, src, rs in ((1, m1, rows), (2, m1, stat), (3, m3, rows))
        ]

    def send(p, b, first, second, edges):
        packed = pack_stats(first, second)
        m1[p, b, 0:16] = packed
        m3[p, b, 0:16] = packed
        if edges is not None:
            m1[p, b, 16:48] = edges(inner)
            m3[p, b, 16:48] = edges(outer)
        for cp in copies(p, b):
            cp.start()

    def receive(p, b):
        for cp in copies(p, b):
            cp.wait_recv()
        parts = [m1[p, b, 0:16]] + [got[p, b, k, 0:16] for k in range(3)]
        first, second = combine_stats(parts, ones[...], entries)
        return first, lax.rsqrt(second - first * first + norm_eps)

    def expand(p, b, affine, own, keep):
        for row in range(pixels // width):
            a = half_silu(affine(own(row)))
            keep[b, pl.ds(row * width, width)] = a.astype(low_type)
            fill_row(abuf, (row + 1) * width, a, channels, width)
        a = half_silu(affine(got[p, b, 0, 16:48].astype(float_type)))
        fill_row(abuf, pl.multiple_of((pixels + width) * (1 - c), width), a, channels, width)
        a = half_silu(affine(got[p, b, 2, 16:48].astype(float_type)))
        a = jnp.where(outer_live, a, 0.0)
        fill_row(abuf, pl.multiple_of((pixels + width) * c, width), a, channels, width)

    def convolve(w):
        depth = 3 * channels
        return sum(
            jnp.dot(
                abuf[width * dy : width * dy + pixels, :],
                w[depth * dy : depth * (dy + 1), :],
                preferred_element_type=float_type,
            )
            for dy in range(3)
        )

    def vec(n):
        return vec_ref[n : n + 1, :]

    pl.semaphore_wait(barrier, 3)

    def step0(b, _):
        v = x_ref[b].astype(float_type)
        send(
            0, b, jnp.sum(v, axis=0, keepdims=True), jnp.sum(v * v, axis=0, keepdims=True),
            lambda at: x_ref[b, pl.ds(at, width)],
        )
        return 0

    lax.fori_loop(0, images, step0, 0)
    load1.wait()

    def step1(b, _):
        centre, scaled = receive(0, b)
        st_ref[b, 0:1] = centre
        st_ref[b, 1:2] = scaled
        slope = scaled * vec(0)
        shift = vec(1)
        expand(
            0, b, lambda v: (v - centre) * slope + shift,
            lambda row: x_ref[b, pl.ds(row * width, width)].astype(float_type), act1_ref,
        )
        hidden = convolve(w1) + vec(2)
        hid_ref[b] = hidden
        send(
            1, b, jnp.sum(hidden, axis=0, keepdims=True),
            jnp.sum(hidden * hidden, axis=0, keepdims=True),
            lambda at: hid_ref[b, pl.ds(at, width)].astype(low_type),
        )
        return 0

    lax.fori_loop(0, images, step1, 0)
    load2.wait()

    def step2(b, _):
        centre, scaled = receive(1, b)
        st_ref[b, 2:3] = centre
        st_ref[b, 3:4] = scaled
        grow = 1.0 + mod_ref[b, 0:1]
        slope = scaled * vec(3) * grow
        shift = vec(4) * grow + mod_ref[b, 1:2]
        expand(
            1, b, lambda v: (v - centre) * slope + shift,
            lambda row: hid_ref[b, pl.ds(row * width, width)], act2_ref,
        )
        middle = (convolve(w2) + vec(5) + x_ref[b].astype(float_type)) * math.sqrt(0.5)
        mid_ref[b] = middle
        send(
            2, b, jnp.sum(middle, axis=0, keepdims=True),
            jnp.sum(middle * middle, axis=0, keepdims=True), None,
        )
        return 0

    lax.fori_loop(0, images, step2, 0)

    def step3(b, _):
        centre, scaled = receive(2, b)
        st_ref[b, 4:5] = centre
        st_ref[b, 5:6] = scaled
        slope = scaled * vec(6)
        att_ref[b] = ((mid_ref[b] - centre) * slope + vec(7)).astype(low_type)
        for p in range(3):
            for cp in copies(p, b):
                cp.wait_send()
        return 0

    lax.fori_loop(0, images, step3, 0)


def forward_call(x, vectors, modulate, first_kernel, second_kernel):
    images, pixels, channels = x.shape
    depth = 9 * channels
    vm = pl.BlockSpec(memory_space=pltpu.VMEM)
    hbm = pl.BlockSpec(memory_space=pl.ANY)
    wide = jax.ShapeDtypeStruct(x.shape, float_type)
    low = jax.ShapeDtypeStruct(x.shape, low_type)
    return pl.pallas_call(
        forward_kernel,
        out_shape=(wide, wide, low, low, low, jax.ShapeDtypeStruct((images, 8, channels), float_type)),
        in_specs=[vm, vm, vm, hbm, hbm],
        out_specs=(vm,) * 6,
        scratch_shapes=[
            pltpu.VMEM((depth, channels), low_type),
            pltpu.VMEM((depth, channels), low_type),
            pltpu.VMEM((channels, channels), low_type),
            pltpu.VMEM((pixels + 64, 3 * channels), low_type),
            pltpu.VMEM((3, images, 48, channels), low_type),
            pltpu.VMEM((3, images, 48, channels), low_type),
            pltpu.VMEM((3, images, 3, 48, channels), low_type),
            pltpu.SemaphoreType.DMA((2,)),
            pltpu.SemaphoreType.DMA((3, images, 3)),
            pltpu.SemaphoreType.DMA((3, images, 3)),
        ],
        compiler_params=pltpu.CompilerParams(
            collective_id=0, has_side_effects=True, vmem_limit_bytes=56 << 20
        ),
        name="forward",
    )(x, vectors, modulate, first_kernel, second_kernel)


def attention_kernel(
    att_ref, mid_ref, cot_ref, vec_ref, jw_any, ow_any,
    res_ref, ag_ref, gj_ref, go_ref, gs_ref,
    jw, ow, att, att_t, kv, kv_t, q8, d_out_t, qm, dom, s_ref, eb, dsb, mix_t, dq_t, dq, dkv,
    part, got_core, to_x, got_x, wsem, gsem, hsem, asem, bsem,
):
    images, pixels, channels = att_ref.shape
    whole = 4 * pixels
    chunk = 128
    pair_lanes = 2 * HEAD
    pairs = channels // pair_lanes
    i, r, c, who = peers()
    loads = [
        pltpu.make_async_copy(jw_any, jw, wsem.at[0]),
        pltpu.make_async_copy(ow_any, ow, wsem.at[1]),
    ]
    for cp in loads:
        cp.start()
    barrier = pltpu.get_barrier_semaphore()
    for k in (1, 2):
        pl.semaphore_signal(barrier, inc=1, device_id=who[k], device_id_type=MESH)

    def block(n):
        return pl.ds(pl.multiple_of(n * pixels, pixels), pixels)

    def shares(b):
        own, far = block(r), block(lax.rem(r + 2, 4))
        return [
            pltpu.make_async_remote_copy(
                att.at[b, rows], att.at[b, rows], gsem.at[b, n], hsem.at[b, n],
                device_id=who[k], device_id_type=MESH,
            )
            for n, (rows, k) in enumerate(((own, 1), (own, 2), (far, 1)))
        ]

    def arrivals(b):
        mate = r + 1 - 2 * c
        rows = (block(mate), block(lax.rem(r + 2, 4)), block(lax.rem(mate + 2, 4)))
        return [
            pltpu.make_async_remote_copy(
                att.at[b, w], att.at[b, w], gsem.at[b, n], hsem.at[b, n],
                device_id=who[(1, 2, 1)[n]], device_id_type=MESH,
            )
            for n, w in enumerate(rows)
        ]

    def forward(b):
        arrivals(b)[1].wait_recv()
        shares(b)[2].start()

    def sums_core(b):
        return [
            pltpu.make_async_remote_copy(
                part.at[b, block(2 * n + 1 - c)], got_core.at[b, n], asem.at[b, n], bsem.at[b, n],
                device_id=who[1], device_id_type=MESH,
            )
            for n in range(2)
        ]

    def sum_x(b):
        return pltpu.make_async_remote_copy(
            to_x.at[b], got_x.at[b], asem.at[b, 2], bsem.at[b, 2],
            device_id=who[2], device_id_type=MESH,
        )

    def pass_on(b):
        x = lax.div(r, 2)
        for cp in sums_core(b):
            cp.wait_recv()
        far = 1 - x
        to_x[b] = (
            part[b, block(2 * far + c)].astype(float_type) + got_core[b, far].astype(float_type)
        ).astype(low_type)
        sum_x(b).start()
        ag_ref[b] = part[b, block(r)].astype(float_type) + got_core[b, x].astype(float_type)

    def keep_own(b, _):
        att[b, block(r)] = att_ref[b]
        return 0

    lax.fori_loop(0, images, keep_own, 0)
    pl.semaphore_wait(barrier, 2)
    for b in range(images):
        shares(b)[0].start()
        shares(b)[1].start()
    for cp in loads:
        cp.wait()
    forward(0)
    lane = lax.broadcasted_iota(jnp.int32, (pixels, pair_lanes), 1)

    def masked(v):
        return jnp.concatenate(
            [jnp.where(lane < HEAD, v, 0.0), jnp.where(lane >= HEAD, v, 0.0)], axis=0
        ).astype(low_type)

    def dot(a, b):
        return jnp.dot(a, b, preferred_element_type=float_type)

    def dot_nt(a, b):
        return lax.dot_general(a, b, contract_cols, preferred_element_type=float_type)

    def one_image(b, _):
        a = arrivals(b)
        a[0].wait_recv()
        a[2].wait_recv()
        bias = jnp.concatenate([jnp.zeros((1, channels), float_type), vec_ref[1:2]], axis=1)
        for n in range(4):
            rows = pl.ds(n * pixels, pixels)
            kv[rows] = (dot(att[b, rows], jw[:, channels:]) + bias).astype(low_type)
        for n in range(2 * channels // 128):
            cols = pl.ds(n * 128, 128)
            kv_t[cols, :] = kv[:, cols].T
        q = (dot(att_ref[b], jw[:, :channels]) + vec_ref[0:1]).astype(low_type)
        q8[...] = (q.astype(float_type) * HEAD ** (-0.5)).astype(low_type)
        d_out = dot_nt(cot_ref[b], ow[...]).astype(low_type).astype(float_type)
        d_out_t[...] = d_out.T

        @pl.when(b > 0)
        def _():
            pass_on(b - 1)

        def one_pair(t, _):
            lanes = pl.ds(pl.multiple_of(t * pair_lanes, pair_lanes), pair_lanes)
            v_lanes = pl.ds(pl.multiple_of(channels + t * pair_lanes, pair_lanes), pair_lanes)
            qm[...] = masked(q8[:, lanes].astype(float_type))
            peak = None
            for n in range(whole // chunk):
                rows = pl.ds(n * chunk, chunk)
                s = dot_nt(kv[rows, lanes], qm[...])
                s_ref[rows] = s
                top = jnp.max(s.reshape(chunk // 8, 8, 2 * pixels), axis=0)
                peak = top if peak is None else jnp.maximum(peak, top)
            peak = jnp.max(peak, axis=0, keepdims=True)
            total = None
            for n in range(whole // chunk):
                rows = pl.ds(n * chunk, chunk)
                e = jnp.exp(s_ref[rows] - peak)
                eb[rows] = e.astype(low_type)
                more = jnp.sum(e.reshape(chunk // 8, 8, 2 * pixels), axis=0)
                total = more if total is None else total + more
            over = 1.0 / jnp.sum(total, axis=0, keepdims=True)
            inner, scaled = [], []
            for j in range(2):
                head = pl.ds(pl.multiple_of(t * pair_lanes + j * HEAD, HEAD), HEAD)
                v_head = pl.ds(pl.multiple_of(channels + t * pair_lanes + j * HEAD, HEAD), HEAD)
                cols = slice(j * pixels, (j + 1) * pixels)
                mt = dot(kv_t[v_head, :], eb[:, cols]) * over[:, cols]
                mix_t[b, head] = mt.astype(low_type)
                g = (d_out_t[head] * over[:, cols]).astype(low_type).astype(float_type)
                inner.append(jnp.sum(g * mt, axis=0, keepdims=True))
                scaled.append(g)
            inner = jnp.concatenate(inner, axis=1)
            dom[...] = masked(jnp.concatenate(scaled, axis=0).T)
            for n in range(whole // chunk):
                rows = pl.ds(n * chunk, chunk)
                dp = dot_nt(kv[rows, v_lanes], dom[...])
                dsb[rows] = (eb[rows].astype(float_type) * (dp - inner)).astype(low_type)
            for j in range(2):
                head = pl.ds(pl.multiple_of(t * pair_lanes + j * HEAD, HEAD), HEAD)
                cols = slice(j * pixels, (j + 1) * pixels)
                dq_t[head] = dot(kv_t[head, :], dsb[:, cols]) * HEAD ** (-0.5)
            dkv[b, :, lanes] = dot(dsb[...], qm[...]).astype(low_type)
            dkv[b, :, v_lanes] = dot(eb[...], dom[...]).astype(low_type)
            return 0

        lax.fori_loop(0, pairs, one_pair, 0)
        dq[b] = dq_t[...].T.astype(low_type)
        for n in range(4):
            rows = pl.ds(n * pixels, pixels)
            part[b, rows] = dot_nt(dkv[b, rows], jw[:, channels:]).astype(low_type)
        part[b, block(r)] = (
            part[b, block(r)].astype(float_type) + dot_nt(dq[b], jw[:, :channels])
        ).astype(low_type)
        for cp in sums_core(b):
            cp.start()

        @pl.when(b + 1 < images)
        def _():
            forward(b + 1)

        mixed = mix_t[b].T
        res_ref[b] = (mid_ref[b] + dot(mixed, ow[...]) + vec_ref[2:3]).astype(low_type)
        return 0

    lax.fori_loop(0, images, one_image, 0)
    pass_on(images - 1)
    ones = jnp.ones((16, whole), low_type)
    for b in range(images):
        att_t[b, 0:channels] = att[b].T
        att_t[b, channels:] = ones
    kv_sum = None
    q_sum = None
    o_sum = None
    for b in range(images):
        more = dot(att_t[b], dkv[b])
        kv_sum = more if kv_sum is None else kv_sum + more
        more = dot(att_t[b, :, block(r)], dq[b])
        q_sum = more if q_sum is None else q_sum + more
        more = dot(mix_t[b], cot_ref[b])
        o_sum = more if o_sum is None else o_sum + more
    gj_ref[:, :channels] = q_sum[:channels]
    gj_ref[:, channels:] = kv_sum[:channels]
    go_ref[...] = o_sum
    cot_sum = jnp.sum(jnp.sum(cot_ref[...].astype(float_type), axis=0), axis=0, keepdims=True)
    gs_ref[0:1] = q_sum[channels : channels + 1]
    gs_ref[1:2] = kv_sum[channels : channels + 1, channels:]
    gs_ref[2:3] = cot_sum
    for b in range(images):
        sum_x(b).wait_recv()
        ag_ref[b] += got_x[b].astype(float_type)
    for b in range(images):
        for cp in shares(b) + sums_core(b) + [sum_x(b)]:
            cp.wait_send()


def attention_call(att, middle, cot, vectors, joint_weight, output_weight):
    images, pixels, channels = att.shape
    whole = 4 * pixels
    vm = pl.BlockSpec(memory_space=pltpu.VMEM)
    hbm = pl.BlockSpec(memory_space=pl.ANY)

    def low(*shape):
        return pltpu.VMEM(shape, low_type)

    def wide(*shape):
        return pltpu.VMEM(shape, float_type)

    return pl.pallas_call(
        attention_kernel,
        out_shape=(
            jax.ShapeDtypeStruct(att.shape, low_type),
            jax.ShapeDtypeStruct(att.shape, float_type),
            jax.ShapeDtypeStruct(joint_weight.shape, float_type),
            jax.ShapeDtypeStruct(output_weight.shape, float_type),
            jax.ShapeDtypeStruct((8, channels), float_type),
        ),
        in_specs=[vm, vm, vm, vm, hbm, hbm],
        out_specs=(vm,) * 5,
        scratch_shapes=[
            low(channels, 3 * channels), low(channels, channels), low(images, whole, channels),
            low(images, channels + 16, whole), low(whole, 2 * channels), low(2 * channels, whole),
            low(pixels, channels), wide(channels, pixels), low(2 * pixels, 2 * HEAD),
            low(2 * pixels, 2 * HEAD), wide(whole, 2 * pixels), low(whole, 2 * pixels),
            low(whole, 2 * pixels), low(images, channels, pixels), wide(channels, pixels),
            low(images, pixels, channels), low(images, whole, 2 * channels),
            low(images, whole, channels), low(images, 2, pixels, channels),
            low(images, pixels, channels), low(images, pixels, channels),
            pltpu.SemaphoreType.DMA((2,)), pltpu.SemaphoreType.DMA((images, 3)),
            pltpu.SemaphoreType.DMA((images, 3)), pltpu.SemaphoreType.DMA((images, 3)),
            pltpu.SemaphoreType.DMA((images, 3)),
        ],
        compiler_params=pltpu.CompilerParams(
            collective_id=1, has_side_effects=True, vmem_limit_bytes=56 << 20
        ),
        name="attention",
    )(att, middle, cot, vectors, joint_weight, output_weight)


def backward_kernel(
    ag_ref, mid_ref, cot_ref, hid_ref, x_ref, act1_ref, act2_ref, st_ref, vec_ref, mod_ref,
    w1_any, w2_any,
    gx_ref, gw1_ref, gw2_ref, mg_ref, gs_ref,
    w1, w2, ones, grad1, grad2, act_t, skip, slope_grad, m1, m3, got, wsem, ssem, rsem,
):
    images, pixels, channels = x_ref.shape
    width = 32
    edge = pixels - width
    span = pixels + 2 * width
    rows_in = pixels // width
    entries = 4.0 * pixels * (channels // GROUPS)
    i, r, c, who = peers()
    loads = [
        pltpu.make_async_copy(w2_any, w2, wsem.at[0]),
        pltpu.make_async_copy(w1_any, w1, wsem.at[1]),
    ]
    for cp in loads:
        cp.start()
    barrier = pltpu.get_barrier_semaphore()
    for k in (1, 2, 3):
        pl.semaphore_signal(barrier, inc=1, device_id=who[k], device_id_type=MESH)
    ones[...] = block_ones(channels, channels // GROUPS)
    gs_ref[...] = jnp.zeros(gs_ref.shape, float_type)
    mg_ref[...] = jnp.zeros(mg_ref.shape, float_type)
    inner = pl.multiple_of(edge * (1 - c), width)
    outer = pl.multiple_of(edge * c, width)
    outer_live = jnp.logical_and(r > 0, r < 3)
    stat = pl.ds(0, 16)
    halo = pl.ds(16, width)
    half = math.sqrt(0.5)

    def stat_copies(p, b):
        return [
            pltpu.make_async_remote_copy(
                m1.at[p, b, stat], got.at[p, b, k - 1, stat], ssem.at[p, b, k - 1],
                rsem.at[p, b, k - 1], device_id=who[k], device_id_type=MESH,
            )
            for k in (1, 2, 3)
        ]

    def halo_copies(p, b):
        return [
            pltpu.make_async_remote_copy(
                src.at[p, b, halo], got.at[p, b, k - 1, halo], ssem.at[p, b, k + 2],
                rsem.at[p, b, k + 2], device_id=who[k], device_id_type=MESH,
            )
            for k, src in ((1, m1), (3, m3))
        ]

    def send_stats(p, b, first, second):
        m1[p, b, 0:16] = pack_stats(first, second)
        for cp in stat_copies(p, b):
            cp.start()

    def receive_stats(p, b):
        for cp in stat_copies(p, b):
            cp.wait_recv()
        parts = [m1[p, b, 0:16]] + [got[p, b, k, 0:16] for k in range(3)]
        return combine_stats(parts, ones[...], entries)

    def send_halo(p, b, buf):
        middle = slice(channels, 2 * channels)
        m1[p, b, 16:48] = buf[b, pl.ds(inner + width, width), middle]
        m3[p, b, 16:48] = buf[b, pl.ds(outer + width, width), middle]
        for cp in halo_copies(p, b):
            cp.start()

    def receive_halo(p, b, buf):
        for cp in halo_copies(p, b):
            cp.wait_recv()
        v = got[p, b, 0, 16:48].astype(float_type)
        fill_row(buf.at[b], pl.multiple_of((pixels + width) * (1 - c), width), v, channels, width)
        v = jnp.where(outer_live, got[p, b, 2, 16:48].astype(float_type), 0.0)
        fill_row(buf.at[b], pl.multiple_of((pixels + width) * c, width), v, channels, width)

    def data_grad(buf, b, w):
        total = None
        for dy in range(3):
            for dx in range(3):
                tap = 3 * dy + dx
                more = lax.dot_general(
                    buf[b, (2 - dy) * width : (2 - dy) * width + pixels,
                        (2 - dx) * channels : (3 - dx) * channels],
                    w[tap * channels : (tap + 1) * channels, :],
                    contract_cols, preferred_element_type=float_type,
                )
                total = more if total is None else total + more
        return total

    def kernel_grad(act_ref, buf, out_ref):
        for b in range(images):
            act_t[:, b * span : b * span + pixels] = act_ref[b].T
        reach = images * span - 2 * width
        flat = buf.reshape(images * span, 3 * channels)
        for dy in range(3):
            g = jnp.dot(
                act_t[:, 0:reach], flat[(2 - dy) * width : (2 - dy) * width + reach, :],
                preferred_element_type=float_type,
            )
            for dx in range(3):
                tap = 3 * dy + dx
                out_ref[tap * channels : (tap + 1) * channels, :] = g[
                    :, (2 - dx) * channels : (3 - dx) * channels
                ].astype(low_type)

    def vec(n):
        return vec_ref[n : n + 1, :]

    def col_sum(v):
        return jnp.sum(v, axis=0, keepdims=True)

    def slope_of(pre):
        s = 0.5 * jnp.tanh(0.5 * pre) + 0.5
        return s * (1.0 + pre * (1.0 - s))

    for b in range(images):
        act_t[:, b * span + pixels : (b + 1) * span] = jnp.zeros((channels, 2 * width), low_type)
    pl.semaphore_wait(barrier, 3)

    def step0(b, _):
        u = ag_ref[b]
        first = col_sum(u)
        second = col_sum(u * ((mid_ref[b] - st_ref[b, 4:5]) * st_ref[b, 5:6]))
        gs_ref[6:7] += second
        gs_ref[7:8] += first
        send_stats(0, b, first * vec(6), second * vec(6))
        return 0

    lax.fori_loop(0, images, step0, 0)

    def step1(b, _):
        first, second = receive_stats(0, b)
        centre, scaled = st_ref[b, 4:5], st_ref[b, 5:6]
        total = jnp.zeros((1, channels), float_type)
        for row in range(rows_in):
            rows = pl.ds(row * width, width)
            normed = (mid_ref[b, rows] - centre) * scaled
            back = scaled * (ag_ref[b, rows] * vec(6) - first - normed * second)
            v = (cot_ref[b, rows].astype(float_type) + back) * half
            skip[b, rows] = v
            v = v.astype(low_type).astype(float_type)
            fill_row(grad2.at[b], (row + 1) * width, v, channels, width)
            total += col_sum(v)
        gs_ref[5:6] += total
        send_halo(1, b, grad2)
        return 0

    lax.fori_loop(0, images, step1, 0)
    loads[0].wait()

    def step2(b, _):
        receive_halo(1, b, grad2)
        upstream = data_grad(grad2, b, w2)
        grow = 1.0 + mod_ref[b, 0:1]
        normed = (hid_ref[b] - st_ref[b, 2:3]) * st_ref[b, 3:4]
        pre = (normed * vec(3) + vec(4)) * grow + mod_ref[b, 1:2]
        v = upstream * slope_of(pre)
        slope_grad[b] = v
        first, second = col_sum(v), col_sum(v * normed)
        mg_ref[b, 0:1] = vec(3) * second + vec(4) * first
        mg_ref[b, 1:2] = first
        first, second = grow * first, grow * second
        gs_ref[3:4] += second
        gs_ref[4:5] += first
        send_stats(2, b, first * vec(3), second * vec(3))
        return 0

    lax.fori_loop(0, images, step2, 0)
    kernel_grad(act2_ref, grad2, gw2_ref)

    def step3(b, _):
        first, second = receive_stats(2, b)
        centre, scaled = st_ref[b, 2:3], st_ref[b, 3:4]
        gain = (1.0 + mod_ref[b, 0:1]) * vec(3)
        total = jnp.zeros((1, channels), float_type)
        for row in range(rows_in):
            rows = pl.ds(row * width, width)
            normed = (hid_ref[b, rows] - centre) * scaled
            v = scaled * (slope_grad[b, rows] * gain - first - normed * second)
            v = v.astype(low_type).astype(float_type)
            fill_row(grad1.at[b], (row + 1) * width, v, channels, width)
            total += col_sum(v)
        gs_ref[2:3] += total
        send_halo(3, b, grad1)
        return 0

    lax.fori_loop(0, images, step3, 0)
    loads[1].wait()

    def step4(b, _):
        receive_halo(3, b, grad1)
        return 0

    lax.fori_loop(0, images, step4, 0)
    kernel_grad(act1_ref, grad1, gw1_ref)

    def step5(b, _):
        upstream = data_grad(grad1, b, w1)
        normed = (x_ref[b].astype(float_type) - st_ref[b, 0:1]) * st_ref[b, 1:2]
        v = upstream * slope_of(normed * vec(0) + vec(1))
        slope_grad[b] = v
        first, second = col_sum(v), col_sum(v * normed)
        gs_ref[0:1] += second
        gs_ref[1:2] += first
        send_stats(4, b, first * vec(0), second * vec(0))
        return 0

    lax.fori_loop(0, images, step5, 0)

    def step6(b, _):
        first, second = receive_stats(4, b)
        scaled = st_ref[b, 1:2]
        normed = (x_ref[b].astype(float_type) - st_ref[b, 0:1]) * scaled
        gx_ref[b] = skip[b] + scaled * (slope_grad[b] * vec(0) - first - normed * second)
        for p in (0, 2, 4):
            for cp in stat_copies(p, b):
                cp.wait_send()
        for p in (1, 3):
            for cp in halo_copies(p, b):
                cp.wait_send()
        return 0

    lax.fori_loop(0, images, step6, 0)


def backward_call(ag, mid, cot, hid, x, act1, act2, stats, vectors, modulate, w1, w2):
    images, pixels, channels = x.shape
    span = pixels + 64
    vm = pl.BlockSpec(memory_space=pltpu.VMEM)
    hbm = pl.BlockSpec(memory_space=pl.ANY)

    def low(*shape):
        return pltpu.VMEM(shape, low_type)

    def wide(*shape):
        return pltpu.VMEM(shape, float_type)

    return pl.pallas_call(
        backward_kernel,
        out_shape=(
            jax.ShapeDtypeStruct(x.shape, float_type),
            jax.ShapeDtypeStruct(w1.shape, low_type),
            jax.ShapeDtypeStruct(w2.shape, low_type),
            jax.ShapeDtypeStruct((images, 8, channels), float_type),
            jax.ShapeDtypeStruct((16, channels), float_type),
        ),
        in_specs=[vm] * 10 + [hbm] * 2,
        out_specs=(vm,) * 5,
        scratch_shapes=[
            low(*w1.shape), low(*w2.shape), low(channels, channels),
            low(images, span, 3 * channels), low(images, span, 3 * channels),
            low(channels, images * span), wide(images, pixels, channels),
            wide(images, pixels, channels), low(5, images, 48, channels),
            low(5, images, 48, channels), low(5, images, 3, 48, channels),
            pltpu.SemaphoreType.DMA((2,)), pltpu.SemaphoreType.DMA((5, images, 6)),
            pltpu.SemaphoreType.DMA((5, images, 6)),
        ],
        compiler_params=pltpu.CompilerParams(
            collective_id=2, has_side_effects=True, vmem_limit_bytes=56 << 20
        ),
        name="backward",
    )(ag, mid, cot, hid, x, act1, act2, stats, vectors, modulate, w1, w2)


def shards(
    images,
    level_count,
    level_index,
    labels,
    first_gain,
    first_shift,
    first_kernel,
    first_offset,
    embed_weight,
    embed_offset,
    class_table,
    second_gain,
    second_shift,
    second_kernel,
    second_offset,
    third_gain,
    third_shift,
    joint_weight,
    joint_offset,
    output_weight,
    output_offset,
    cotangent,
):
    image_count, stripe_rows, image_width, channels = images.shape
    layout = (image_count, stripe_rows, image_width, channels)
    pixels = stripe_rows * image_width
    gain_one = first_gain.astype(float_type)
    shift_one = first_shift.astype(float_type)
    gain_two = second_gain.astype(float_type)
    shift_two = second_shift.astype(float_type)
    gain_three = third_gain.astype(float_type)
    features = noise_features(level_count, level_index)
    class_count = class_table.shape[0]
    one_hot = (labels[:, None] == jnp.arange(class_count, dtype=jnp.int32)[None, :]).astype(
        low_type
    )
    embedded = features + jnp.dot(one_hot, class_table, preferred_element_type=float_type)
    embed_act = jax.nn.silu(embedded).astype(low_type)
    modulate = jnp.dot(
        embed_act, embed_weight, preferred_element_type=float_type
    ) + embed_offset.astype(float_type)
    scale_part = modulate[:, :channels]
    vectors = jnp.stack(
        [
            first_gain, first_shift, first_offset, second_gain, second_shift, second_offset,
            third_gain, third_shift,
        ]
    ).astype(float_type)
    x = images.reshape(image_count, pixels, channels)
    hidden, middle, attend, act_one, act_two, stats = forward_call(
        x, vectors, modulate.reshape(image_count, 2, channels), first_kernel, second_kernel
    )
    attention_vectors = jnp.stack(
        [joint_offset[:channels], joint_offset[channels:], output_offset]
    ).astype(float_type)
    cot = cotangent.reshape(image_count, pixels, channels)
    result, attend_grad, joint_weight_grad, output_weight_grad, sums = attention_call(
        attend, middle, cot, attention_vectors, joint_weight, output_weight
    )
    result = result.reshape(layout)
    joint_offset_grad = jnp.concatenate([sums[0], sums[1]])
    output_offset_grad = sums[2]
    images_gradient, first_kernel_grad, second_kernel_grad, modulate_grad, sums = backward_call(
        attend_grad, middle, cot, hidden, x, act_one, act_two, stats, vectors,
        modulate.reshape(image_count, 2, channels), first_kernel, second_kernel,
    )
    images_gradient = images_gradient.reshape(layout)
    (
        first_gain_grad, first_shift_grad, first_offset_grad, second_gain_grad, second_shift_grad,
        second_offset_grad, third_gain_grad, third_shift_grad,
    ) = (sums[n] for n in range(8))
    modulate_grad = modulate_grad[:, :2].reshape(image_count, 2 * channels)
    modulate_grad = lax.psum(modulate_grad, "row")
    every_grad, every_embedded, every_label = lax.all_gather(
        (modulate_grad, embedded, labels), "img", axis=0, tiled=True
    )
    stripe_index = lax.axis_index("row")
    stripe_count = lax.axis_size("row")

    def own_rows(v, axis):
        size = v.shape[axis] // stripe_count
        return lax.dynamic_slice_in_dim(v, stripe_index * size, size, axis)

    every_act = jax.nn.silu(every_embedded).astype(low_type).astype(float_type)
    embed_weight_grad = lax.dot_general(
        own_rows(every_act, 1), every_grad, contract_rows, precision=highest
    )
    embed_offset_grad = own_rows(jnp.sum(every_grad, axis=0), 0)
    active_grad = lax.dot_general(
        every_grad, embed_weight.astype(float_type), contract_cols, precision=highest
    )
    embedded_grad = active_grad * silu_slope(every_embedded)
    own_classes = stripe_index * (class_count // stripe_count) + jnp.arange(
        class_count // stripe_count, dtype=jnp.int32
    )
    own_hot = (every_label[:, None] == own_classes[None, :]).astype(float_type)
    class_table_grad = lax.dot_general(own_hot, embedded_grad, contract_rows, precision=highest)

    def scattered(v):
        v = lax.psum_scatter(v.astype(low_type), "row", scatter_dimension=0, tiled=True)
        return lax.psum(v.astype(low_type), "img").astype(float_type)

    first_kernel_grad, second_kernel_grad, joint_weight_grad, output_weight_grad = (
        scattered(v)
        for v in (first_kernel_grad, second_kernel_grad, joint_weight_grad, output_weight_grad)
    )
    small = (
        first_gain_grad, first_shift_grad, first_offset_grad, second_gain_grad, second_shift_grad,
        second_offset_grad, third_gain_grad, third_shift_grad, joint_offset_grad,
        output_offset_grad,
    )
    summed = lax.psum(jnp.concatenate(small), ("img", "row"))
    pieces, at = [], 0
    for v in small:
        pieces.append(own_rows(summed[at : at + v.shape[0]], 0))
        at += v.shape[0]
    (
        first_gain_grad, first_shift_grad, first_offset_grad, second_gain_grad, second_shift_grad,
        second_offset_grad, third_gain_grad, third_shift_grad, joint_offset_grad,
        output_offset_grad,
    ) = pieces
    return (
        result, images_gradient, first_gain_grad, first_shift_grad, first_kernel_grad,
        first_offset_grad, embed_weight_grad, embed_offset_grad, class_table_grad,
        second_gain_grad, second_shift_grad, second_kernel_grad, second_offset_grad,
        third_gain_grad, third_shift_grad, joint_weight_grad, joint_offset_grad,
        output_weight_grad, output_offset_grad,
    )


def solution(mesh):
    in_specs = (
        (P("img", "row", None, None),) + (P("img"),) * 3 + (P(),) * 17
        + (P("img", "row", None, None),)
    )
    row, rows = P("row"), P("row", None)
    out_specs = (
        P("img", "row", None, None), P("img", "row", None, None), row, row, rows, row, rows, row,
        rows, row, row, rows, row, row, row, rows, row, rows, row,
    )
    return jax.shard_map(shards, mesh=mesh, in_specs=in_specs, out_specs=out_specs, check_vma=False)
```

profile of v0, /device:TPU:0, one launch (start us, length us, event | category | flops | bytes accessed | tf_op | source)
XLA Modules:
  0.0 365.4 jit_solution(7382158197721480451)
XLA Ops:
  7.3 0.8 stack.39
  8.1 0.7 stack.40
  8.8 0.7 stack.41
  9.5 0.7 stack.42
  13.6 0.8 fusion.14
  14.3 0.7 convert_element_type.47
  15.7 0.7 log_multiply_fusion
  16.5 1.0 convolution_add_fusion
  19.0 21.9 %forward.1 = (f32[3,256,384]{2,1,0:T(8,128)}, f32[3,256,384]{2,1,0:T(8,128)}, bf16[3,256,384]{2,1,0:T(8,128)(2,1)}, bf16[3,256,384]{2,1,0:T(8,128)(2,1)}, bf16[3...) custom-call(bf16[3,256,384]{2,1,0:T(8,128)(2,1)} %bitcast.16, f32[8,384]{1,0:T(8,128)} %convert_element_type.43.vec_ref, ...), custom_call_target="tpu_custom_call" | custom-call | tf_op jit(solution)/shard_map/forward/pallas_call | solution.py:308
  40.9 52.1 %attention.1 = (bf16[3,256,384]{2,1,0:T(8,128)(2,1)}, f32[3,256,384]{2,1,0:T(8,128)}, f32[384,1152]{1,0:T(8,128)}, f32[384,384]{1,0:T(8,128)}, f32[8,384]{1,0:T(8,128)}) custom-call(bf16[3,256,384]{2,1,0:T(8,128)(2,1)} %get-tuple-element.35.att_ref, f32[3,256,384]{2,1,0:T(8,128)} %get-tuple-element.36.mid_ref, bf16[3,256,384]{2,1,0:T(8,128)(2,1)} %bitcast.18, ...), custom_call_target="tpu_custom_call" | custom-call | tf_op jit(solution)/shard_map/attention/pallas_call | solution.py:559
  93.0 1.8 convert_element_type.54
  94.9 2.5 convert_element_type.52
  97.6 36.1 %backward.1 = (f32[3,256,384]{2,1,0:T(8,128)}, bf16[3456,384]{1,0:T(8,128)(2,1)}, bf16[3456,384]{1,0:T(8,128)(2,1)}, f32[3,8,384]{2,1,0:T(8,128)}, f32[16,384]{1,0:T(8,128)}) custom-call(f32[3,256,384]{2,1,0:T(8,128)} %get-tuple-element.38.ag_ref, f32[3,256,384]{2,1,0:T(8,128)} %get-tuple-element.36.mid_ref, bf16[3,256,384]{2,1,0:T(8,128)(2,1)} %bitcast.19, ...), custom_call_target="tpu_custom_call" | custom-call | tf_op jit(solution)/shard_map/backward/pallas_call | solution.py:828
  136.1 0.8 slice_reduce_fusion
  136.9 0.8 slice_bitcast_fusion
  137.7 6.2 %reduce-scatter.9.cloned.1.call-done = bf16[96,1152]{1,0:T(8,128)(2,1)} async-done(((bf16[384,1152]{1,0:T(8,128)(2,1)}), bf16[96,1152]{1,0:T(8,128)(2,1)}) %reduce-scatter.9.cloned.1.call-update) | async-done | bytes 221200 | tf_op jit(solution)/shard_map/reduce_scatter | solution.py:955
  143.9 37.5 %reduce-scatter.5.cloned.1.call-done = bf16[864,384]{1,0:T(8,128)(2,1)} async-done(((bf16[3456,384]{1,0:T(8,128)(2,1)}), bf16[864,384]{1,0:T(8,128)(2,1)}) %reduce-scatter.5.cloned.1.call-update) | async-done | bytes 663568 | tf_op jit(solution)/shard_map/reduce_scatter | solution.py:955
  181.4 37.5 %reduce-scatter.7.cloned.1.call-done = bf16[864,384]{1,0:T(8,128)(2,1)} async-done(((bf16[3456,384]{1,0:T(8,128)(2,1)}), bf16[864,384]{1,0:T(8,128)(2,1)}) %reduce-scatter.7.cloned.1.call-update) | async-done | bytes 663568 | tf_op jit(solution)/shard_map/reduce_scatter | solution.py:955
  218.9 11.5 %all-reduce = s32[24]{0:T(128)S(1)} all-reduce(s32[24]{0:T(128)S(1)} %dynamic-update-slice), channel_id=1, replica_groups=mesh['img'=8,'row'=4] {'img'}, use_global_device_ids=true, to_apply=%add | all-reduce | flops 24 | bytes 192
  230.4 31.2 %all-gather = f32[8,3,768]{2,1,0:T(4,128)S(1)} all-gather(f32[1,3,768]{2,1,0:T(4,128)S(1)} %bitcast.22), channel_id=1, replica_groups=mesh['img'=8,'row'=4] {'img'}, dimensions={0}, use_global_device_ids=true | all-gather | bytes 82944 | tf_op jit(solution)/shard_map/all_gather | solution.py:929
  261.6 37.6 %psum.42 = f32[4224]{0:T(1024)S(1)} all-reduce(f32[4224]{0:T(1024)S(1)} %constant_dynamic-update-slice_fusion), channel_id=1, replica_groups=mesh['img'=8,'row'=4] {'img','row'}, use_global_device_ids=true, to_apply=%region_0.1 | all-reduce | flops 4224 | bytes 33792 | tf_op jit(solution)/shard_map/psum | solution.py:967
  304.5 11.0 %psum.44 = f32[3,768]{1,0:T(4,128)S(1)} all-reduce(f32[3,768]{1,0:T(4,128)S(1)} %bitcast.24), channel_id=1, replica_groups=mesh['img'=8,'row'=4] {'row'}, use_global_device_ids=true, to_apply=%region_3.4 | all-reduce | flops 2304 | bytes 18432 | tf_op jit(solution)/shard_map/psum | solution.py:928
  315.5 30.5 %all-gather.1 = f32[8,3,768]{2,1,0:T(4,128)S(1)} all-gather(f32[1,3,768]{2,1,0:T(4,128)S(1)} %bitcast.23), channel_id=1, replica_groups=mesh['img'=8,'row'=4] {'img'}, dimensions={0}, use_global_device_ids=true | all-gather | bytes 82944 | tf_op jit(solution)/shard_map/all_gather | solution.py:929
  347.4 1.3 fusion.3
  348.7 1.1 convolution_multiply_fusion
  349.8 1.5 fusion.1
  351.3 1.6 convert_element_type.55
  352.9 1.8 convert_element_type.53
  354.7 1.1 convert_element_type.49
  355.9 1.1 convert_element_type.51
  357.1 0.8 copy.60
  357.9 1.0 copy.61
  (79 shorter events, 14.4 us)
Async XLA Ops:
  7.2 9.3 %copy-start = (bf16[1000,768]{1,0:T(8,128)(2,1)S(1)}, bf16[1000,768]{1,0:T(8,128)(2,1)}, u32[]{:S(2)}) copy-start(bf16[1000,768]{1,0:T(8,128)(2,1)} %param.32) | copy-start | bytes 4608004
  7.2 10.3 %copy-start.1 = (bf16[768,768]{1,0:T(8,128)(2,1)S(1)}, bf16[768,768]{1,0:T(8,128)(2,1)}, u32[]{:S(2)}) copy-start(bf16[768,768]{1,0:T(8,128)(2,1)} %param.30) | copy-start | bytes 3538948
  7.2 130.5 %reduce-scatter.11.cloned.1.call-start = ((), (), s32[]{:S(2)}) async-start(), calls=%async_computation.7 | async-start | bytes 368640 | tf_op jit(solution)/shard_map/reduce_scatter | solution.py:955
  94.8 49.1 %reduce-scatter.9.cloned.1.call-start = ((), (), s32[]{:S(2)}) async-start(), calls=%async_computation.6 | async-start | bytes 1105920 | tf_op jit(solution)/shard_map/reduce_scatter | solution.py:955
  97.4 84.0 %reduce-scatter.5.cloned.1.call-start = ((), (), s32[]{:S(2)}) async-start(), calls=%async_computation.4 | async-start | bytes 3317760 | tf_op jit(solution)/shard_map/reduce_scatter | solution.py:955
  133.7 85.2 %reduce-scatter.7.cloned.1.call-start = ((), (), s32[]{:S(2)}) async-start(), calls=%async_computation.5 | async-start | bytes 3317760 | tf_op jit(solution)/shard_map/reduce_scatter | solution.py:955
  133.8 0.7 copy-start.8
  133.8 1.9 copy-start.7
  133.8 2.1 copy-start.6
  134.3 217.0 %all-reduce.4.cloned.1.call-start = ((), (), s32[]{:S(2)}) async-start(), calls=%async_computation.8 | async-start | bytes 3244032 | tf_op jit(solution)/shard_map/psum | solution.py:956
  351.3 3.4 copy-start.4
  352.9 3.0 copy-start.3
  355.9 1.2 copy-start.5
  355.9 2.0 copy-start.2
Sparse Core Ops, SparseCore 0:
  94.9 21.5 reduce-scatter.10
  119.8 24.0 reduce-scatter.8
  146.5 34.9 reduce-scatter.4
  184.0 34.8 reduce-scatter.6
  222.7 92.2 all-reduce.3
where the time goes:
time: 366 us; the launch traced here: 365 us
  blocking collectives  122 us (33%)
  Pallas kernels  110 us (30%)
  waiting for transfers between devices  81.7 us (22%)
  local copies, waits for them, and re-layouts  18.9 us (5%)
  between operations  14.7 us (4%)
  other arithmetic  12.8 us (3%)
  matrix products  5.15 us (1%)
    reduce_scatter x4, waiting for transfers between devices, scattered(): lax.psum_scatter(v.astype(low_type), 'row', scatter_dimension=0, tiled=True)  81.2 us
    all_gather x2, blocking collectives, shards(): lax.all_gather((modulate_grad, embedded, labels), 'img', axis=0, tiled=True)  61.7 us
    pallas_call x1, Pallas kernels, attention_call(): pl.pallas_call(attention_kernel, out_shape=(jax.ShapeDtypeStruct(att.shap...  52.1 us
    psum x1, blocking collectives, shards(): summed = lax.psum(jnp.concatenate(small), ('img', 'row'))  37.6 us
    pallas_call x1, Pallas kernels, backward_call(): pl.pallas_call(backward_kernel, out_shape=(jax.ShapeDtypeStruct(x.shape,...  36.1 us
    pallas_call x1, Pallas kernels, forward_call(): pl.pallas_call(forward_kernel, out_shape=(wide, wide, low, low, low, jax....  21.9 us
    unnamed x1, blocking collectives  11.5 us
    psum x1, blocking collectives, shards(): modulate_grad = lax.psum(modulate_grad, 'row')  11 us
  transfers between devices with their start and end apart: 5, of which 3 were waited for; matrix products, arithmetic and copies ran while one was open for 4% of the time, Pallas kernels for 10%

commit v1 on v0

--- a/solution.py
+++ b/solution.py
@@ -331,7 +331,7 @@
 
 def attention_kernel(
     att_ref, mid_ref, cot_ref, vec_ref, jw_any, ow_any,
-    res_ref, ag_ref, gj_ref, go_ref, gs_ref,
+    res_ref, ag_ref, gjo_ref, gs_ref,
     jw, ow, att, att_t, kv, kv_t, q8, d_out_t, qm, dom, s_ref, eb, dsb, mix_t, dq_t, dq, dkv,
     part, got_core, to_x, got_x, wsem, gsem, hsem, asem, bsem,
 ):
@@ -529,9 +529,13 @@
         q_sum = more if q_sum is None else q_sum + more
         more = dot(mix_t[b], cot_ref[b])
         o_sum = more if o_sum is None else o_sum + more
-    gj_ref[:, :channels] = q_sum[:channels]
-    gj_ref[:, channels:] = kv_sum[:channels]
-    go_ref[...] = o_sum
+    part_rows = channels // 4
+    every = (q_sum, kv_sum[:, :channels], kv_sum[:, channels:], o_sum)
+    for n, v in enumerate(every):
+        for m in range(4):
+            gjo_ref[m, n * part_rows : (n + 1) * part_rows] = v[
+                m * part_rows : (m + 1) * part_rows
+            ].astype(low_type)
     cot_sum = jnp.sum(jnp.sum(cot_ref[...].astype(float_type), axis=0), axis=0, keepdims=True)
     gs_ref[0:1] = q_sum[channels : channels + 1]
     gs_ref[1:2] = kv_sum[channels : channels + 1, channels:]
@@ -561,12 +565,11 @@
         out_shape=(
             jax.ShapeDtypeStruct(att.shape, low_type),
             jax.ShapeDtypeStruct(att.shape, float_type),
-            jax.ShapeDtypeStruct(joint_weight.shape, float_type),
-            jax.ShapeDtypeStruct(output_weight.shape, float_type),
+            jax.ShapeDtypeStruct((4, channels, channels), low_type),
             jax.ShapeDtypeStruct((8, channels), float_type),
         ),
         in_specs=[vm, vm, vm, vm, hbm, hbm],
-        out_specs=(vm,) * 5,
+        out_specs=(vm,) * 4,
         scratch_shapes=[
             low(channels, 3 * channels), low(channels, channels), low(images, whole, channels),
             low(images, channels + 16, whole), low(whole, 2 * channels), low(2 * channels, whole),
@@ -587,11 +590,153 @@
     )(att, middle, cot, vectors, joint_weight, output_weight)
 
 
+def chip_peers(i, r):
+    size = lax.axis_size("img")
+    z = lax.rem(lax.div(i, 2), 4)
+    e = lax.div(i, 8)
+    others = (z + 1 - 2 * lax.rem(z, 2), lax.rem(z + 2, 4), 3 - z)
+    more = size // 8
+    return {
+        "y": [(i + 1 - 2 * lax.rem(i, 2), r)],
+        "z": [(i + 2 * (n - z), r) for n in others],
+        "e": [(i + 8 * (lax.rem(e + k, more) - e), r) for k in range(1, more)],
+        "at": (lax.rem(i, 2), z),
+        "pieces": others,
+    }
+
+
+class Reduction:
+    def __init__(self, out, lanes, n, q, refs, who, place, cs, cr, es, er):
+        if n is not None:
+            refs = (refs[0].at[n],) + tuple(ref.at[n] for ref in refs[1:])
+        (self.grad, self.got_core, self.to_x, self.got_x, self.own, self.to_y, self.got_y,
+         self.to_z, self.got_z, self.got_e) = refs
+        self.out, self.lanes, self.q, self.who = out, lanes, q, who
+        self.c, self.x, self.chips = place
+        self.y, self.z = self.chips["at"]
+        self.sems = (cs, cr, es, er)
+        self.size = self.own.shape[0]
+
+    def copy(self, src, dst, n, at, extra=False):
+        send, recv = self.sems[2:] if extra else self.sems[:2]
+        return pltpu.make_async_remote_copy(
+            src, dst, send.at[self.q, n], recv.at[self.q, n], device_id=at, device_id_type=MESH
+        )
+
+    def half(self, y):
+        size = self.size // 2
+        return pl.ds(pl.multiple_of(y * size, size), size)
+
+    def piece(self, z, y=0):
+        size = self.size // 8
+        return pl.ds(pl.multiple_of(y * (self.size // 2) + z * size, size), size)
+
+    def core_copies(self):
+        return [
+            self.copy(self.grad.at[2 * n + 1 - self.c], self.got_core.at[n], n, self.who[1])
+            for n in range(2)
+        ]
+
+    def x_copies(self):
+        return [self.copy(self.to_x, self.got_x, 2, self.who[2])]
+
+    def y_copies(self):
+        return [self.copy(self.to_y, self.got_y, 3, self.chips["y"][0])]
+
+    def z_copies(self):
+        return [
+            self.copy(self.to_z.at[self.piece(p)], self.got_z.at[n], 4 + n, at)
+            for n, (p, at) in enumerate(zip(self.chips["pieces"], self.chips["z"]))
+        ]
+
+    def extra_copies(self):
+        src = self.to_z.at[self.piece(self.z)]
+        return [
+            self.copy(src, self.got_e.at[n], n, at, True) for n, at in enumerate(self.chips["e"])
+        ]
+
+    def back_z_copies(self):
+        part = self.out.at[self.piece(self.z, self.y), self.lanes]
+        return [self.copy(part, part, 7 + n, at) for n, at in enumerate(self.chips["z"])]
+
+    def back_y_copies(self):
+        part = self.out.at[self.half(self.y), self.lanes]
+        return [self.copy(part, part, 10, self.chips["y"][0])]
+
+    def core(self):
+        for cp in self.core_copies():
+            cp.start()
+
+    def across_x(self):
+        for cp in self.core_copies():
+            cp.wait_recv()
+        far = 1 - self.x
+        self.to_x[...] = (
+            self.grad[2 * far + self.c].astype(float_type) + self.got_core[far].astype(float_type)
+        ).astype(low_type)
+        self.x_copies()[0].start()
+        self.own[...] = self.grad[2 * self.x + self.c].astype(float_type) + self.got_core[
+            self.x
+        ].astype(float_type)
+
+    def across_y(self):
+        self.x_copies()[0].wait_recv()
+        self.own[...] += self.got_x[...].astype(float_type)
+        self.to_y[...] = self.own[self.half(1 - self.y)].astype(low_type)
+        self.y_copies()[0].start()
+
+    def across_z(self):
+        self.y_copies()[0].wait_recv()
+        rows = self.half(self.y)
+        v = self.own[rows] + self.got_y[...].astype(float_type)
+        self.own[rows] = v
+        self.to_z[...] = v.astype(low_type)
+        for cp in self.z_copies():
+            cp.start()
+
+    def back_z(self):
+        for cp in self.z_copies():
+            cp.wait_recv()
+        rows = self.piece(self.z, self.y)
+        v = self.own[rows]
+        for n in range(3):
+            v = v + self.got_z[n].astype(float_type)
+        if self.chips["e"]:
+            self.to_z[self.piece(self.z)] = v.astype(low_type)
+            for cp in self.extra_copies():
+                cp.start()
+            for n, cp in enumerate(self.extra_copies()):
+                cp.wait_recv()
+                v = v + self.got_e[n].astype(float_type)
+        self.out[rows, self.lanes] = v.astype(low_type)
+        for cp in self.back_z_copies():
+            cp.start()
+
+    def back_y(self):
+        for cp in self.back_z_copies():
+            cp.wait_recv()
+        self.back_y_copies()[0].start()
+
+    def end(self):
+        self.back_y_copies()[0].wait_recv()
+
+    def drain(self):
+        for cp in (
+            self.core_copies() + self.x_copies() + self.y_copies() + self.z_copies()
+            + self.extra_copies() + self.back_z_copies() + self.back_y_copies()
+        ):
+            cp.wait_send()
+
+
 def backward_kernel(
     ag_ref, mid_ref, cot_ref, hid_ref, x_ref, act1_ref, act2_ref, st_ref, vec_ref, mod_ref,
-    w1_any, w2_any,
-    gx_ref, gw1_ref, gw2_ref, mg_ref, gs_ref,
-    w1, w2, ones, grad1, grad2, act_t, skip, slope_grad, m1, m3, got, wsem, ssem, rsem,
+    gjo_ref, sums_ref, emb_ref, w1_any, w2_any, ew_any,
+    gx_ref, gw1_ref, gw2_ref, go_ref, gv_ref, ge_ref, gc_ref, geo_ref,
+    w1, w2, ew, ones, grad1, grad2, act_t, skip, slope_grad, m1, m3, got, gs_ref, mg_ref,
+    gw, w_core, w_to_x, w_got_x, w_own, w_to_y, w_got_y, w_to_z, w_got_z, w_got_e,
+    o_core, o_to_x, o_got_x, o_own, o_to_y, o_got_y, o_to_z, o_got_z, o_got_e,
+    v_own, v_row, v_one, v_y, v_two, v_z, v_three, v_e, g_row, gat, left, hot,
+    wsem, ssem, rsem, cs, cr, es, er, vs, vr, gsem, hsem,
 ):
     images, pixels, channels = x_ref.shape
     width = 32
@@ -603,21 +748,39 @@
     loads = [
         pltpu.make_async_copy(w2_any, w2, wsem.at[0]),
         pltpu.make_async_copy(w1_any, w1, wsem.at[1]),
+        pltpu.make_async_copy(ew_any, ew, wsem.at[2]),
     ]
     for cp in loads:
         cp.start()
     barrier = pltpu.get_barrier_semaphore()
-    for k in (1, 2, 3):
-        pl.semaphore_signal(barrier, inc=1, device_id=who[k], device_id_type=MESH)
+    chips = chip_peers(i, r)
+    greeted = list(who.values()) + chips["y"] + chips["z"] + chips["e"]
+    for at in greeted:
+        pl.semaphore_signal(barrier, inc=1, device_id=at, device_id_type=MESH)
+    place = (c, lax.div(r, 2), chips)
     ones[...] = block_ones(channels, channels // GROUPS)
     gs_ref[...] = jnp.zeros(gs_ref.shape, float_type)
+    quarter = 9 * channels // 4
+    padded = gw.shape[2]
     mg_ref[...] = jnp.zeros(mg_ref.shape, float_type)
+    for n in range(6):
+        for m in range(4):
+            gw[n, m, quarter:padded] = jnp.zeros((padded - quarter, 128), low_type)
     inner = pl.multiple_of(edge * (1 - c), width)
     outer = pl.multiple_of(edge * c, width)
     outer_live = jnp.logical_and(r > 0, r < 3)
     stat = pl.ds(0, 16)
     halo = pl.ds(16, width)
     half = math.sqrt(0.5)
+
+    def chunk(out, lanes, n, q, refs):
+        return Reduction(out, lanes, n, q, refs, who, place, cs, cr, es, er)
+
+    refs = (gw, w_core, w_to_x, w_got_x, w_own, w_to_y, w_got_y, w_to_z, w_got_z, w_got_e)
+    red2 = [chunk(gw2_ref, slice(128 * n, 128 * n + 128), n, n, refs) for n in range(3)]
+    red1 = [chunk(gw1_ref, slice(128 * n, 128 * n + 128), n + 3, n + 3, refs) for n in range(3)]
+    refs = (gjo_ref, o_core, o_to_x, o_got_x, o_own, o_to_y, o_got_y, o_to_z, o_got_z, o_got_e)
+    red0 = chunk(go_ref, slice(0, channels), None, 6, refs)
 
     def stat_copies(p, b):
         return [
@@ -677,7 +840,7 @@
                 total = more if total is None else total + more
         return total
 
-    def kernel_grad(act_ref, buf, out_ref):
+    def kernel_grad(act_ref, buf, base):
         for b in range(images):
             act_t[:, b * span : b * span + pixels] = act_ref[b].T
         reach = images * span - 2 * width
@@ -689,9 +852,152 @@
             )
             for dx in range(3):
                 tap = 3 * dy + dx
-                out_ref[tap * channels : (tap + 1) * channels, :] = g[
-                    :, (2 - dx) * channels : (3 - dx) * channels
-                ].astype(low_type)
+                at = (2 - dx) * channels
+                for m in range(4):
+                    lo = max(tap * channels, m * quarter)
+                    hi = min((tap + 1) * channels, (m + 1) * quarter)
+                    for n in range(3 if lo < hi else 0):
+                        gw[base + n, m, lo - m * quarter : hi - m * quarter] = g[
+                            lo - tap * channels : hi - tap * channels,
+                            at + 128 * n : at + 128 * n + 128,
+                        ].astype(low_type)
+
+    def remote(src, dst, send, recv, at):
+        return pltpu.make_async_remote_copy(
+            src, dst, send, recv, device_id=at, device_id_type=MESH
+        )
+
+    def start(copies):
+        for cp in copies:
+            cp.start()
+
+    def arrived(copies):
+        for cp in copies:
+            cp.wait_recv()
+
+    zs, extras = chips["z"], chips["e"]
+
+    def small_row_copies(s):
+        return [
+            remote(v_own.at[s], v_row.at[s, k - 1], vs.at[s, k - 1], vr.at[s, k - 1], who[k])
+            for k in (1, 2, 3)
+        ]
+
+    def small_y_copies(s):
+        return [remote(v_one.at[s], v_y.at[s], vs.at[s, 3], vr.at[s, 3], chips["y"][0])]
+
+    def small_z_copies(s):
+        return [
+            remote(v_two.at[s], v_z.at[s, n], vs.at[s, 4 + n], vr.at[s, 4 + n], at)
+            for n, at in enumerate(zs)
+        ]
+
+    def small_e_copies(s):
+        return [
+            remote(v_three.at[s], v_e.at[s, n], vs.at[s, 7 + n], vr.at[s, 7 + n], at)
+            for n, at in enumerate(extras)
+        ]
+
+    def small_row(s):
+        v_own[s] = gs_ref[...]
+        start(small_row_copies(s))
+
+    def small_y(s):
+        arrived(small_row_copies(s))
+        v_one[s] = v_own[s] + v_row[s, 0] + v_row[s, 1] + v_row[s, 2]
+        start(small_y_copies(s))
+
+    def small_z(s):
+        arrived(small_y_copies(s))
+        v_two[s] = v_one[s] + v_y[s]
+        start(small_z_copies(s))
+
+    def small_end(s):
+        arrived(small_z_copies(s))
+        v_three[s] = v_two[s] + v_z[s, 0] + v_z[s, 1] + v_z[s, 2]
+        total = v_three[s]
+        if extras:
+            start(small_e_copies(s))
+            arrived(small_e_copies(s))
+            for n in range(len(extras)):
+                total = total + v_e[s, n]
+        gv_ref[s] = total
+
+    def gather_row_copies():
+        return [
+            remote(mg_ref, g_row.at[k - 1], gsem.at[k - 1], hsem.at[k - 1], who[k])
+            for k in (1, 2, 3)
+        ]
+
+    def gather_copies():
+        blocks = [pl.ds(i, 1), pl.ds(pl.multiple_of(i - lax.rem(i, 2), 2), 2)]
+        blocks.append(pl.ds(pl.multiple_of(i - lax.rem(i, 8), 8), 8))
+        found = []
+        for rows, places in zip(blocks, (chips["y"], zs, extras)):
+            for at in places:
+                n = 3 + len(found)
+                found.append(remote(gat.at[rows], gat.at[rows], gsem.at[n], hsem.at[n], at))
+        return found
+
+    def gather_row():
+        start(gather_row_copies())
+
+    def gather_y():
+        arrived(gather_row_copies())
+        gat[i] = emb_ref[...] + mg_ref[...] + g_row[0] + g_row[1] + g_row[2]
+        start(gather_copies()[:1])
+
+    def gather_z():
+        arrived(gather_copies()[:1])
+        start(gather_copies()[1:4])
+
+    def gather_end():
+        arrived(gather_copies()[1:4])
+        start(gather_copies()[4:])
+        arrived(gather_copies()[4:])
+
+    def three_terms(v):
+        a = v.astype(low_type)
+        b = (v - a.astype(float_type)).astype(low_type)
+        d = (v - a.astype(float_type) - b.astype(float_type)).astype(low_type)
+        return jnp.concatenate([a, b, d], axis=0)
+
+    def embedding():
+        ge_ref[...] = jnp.zeros(ge_ref.shape, float_type)
+        gc_ref[...] = jnp.zeros(gc_ref.shape, float_type)
+        geo_ref[...] = jnp.zeros(geo_ref.shape, float_type)
+        lax.fori_loop(0, gat.shape[0] // 8, embedding_part, 0)
+
+    def embedding_part(part_of, _):
+        every = 64
+        full = gat[pl.ds(pl.multiple_of(part_of * 8, 8), 8)].reshape(every, 2 * channels)
+        place_of = lax.rem(lax.broadcasted_iota(jnp.int32, (every, 2 * channels), 0), 8)
+        live = place_of < images
+        grad = jnp.where(live, full, 0.0)
+        held = jnp.where(live, pltpu.roll(full, every - images, 0), 0.0)
+        act = jnp.where(live, half_silu(held), 0.0).astype(low_type)
+        left[...] = jnp.concatenate([act, act, act], axis=0).T
+        terms = three_terms(grad)
+        size = 2 * channels // 4
+        own = pl.ds(pl.multiple_of(r * size, size), size)
+        ge_ref[...] += jnp.dot(left[own, :], terms, preferred_element_type=float_type)
+        geo_ref[...] += jnp.broadcast_to(jnp.sum(grad, axis=0, keepdims=True), geo_ref.shape)
+        active = lax.dot_general(terms, ew[...], contract_cols, preferred_element_type=float_type)
+        active = active[0:every] + active[every : 2 * every] + active[2 * every :]
+        back = jnp.where(live, active * slope_of(held), 0.0)
+        classes = gc_ref.shape[0]
+        row_of = lax.rem(lax.broadcasted_iota(jnp.int32, (every, 128), 0), 8)
+        label = jnp.full((every, 128), -1.0, float_type)
+        for b in range(images):
+            rolled = pltpu.roll(full[:, 256 * b : 256 * b + 128], every - 2 * images + b, 0)
+            label = jnp.where(row_of == b, rolled, label)
+        for n in range(hot.shape[0] // 128):
+            kind = lax.broadcasted_iota(jnp.int32, (every, 128), 1) + 128 * n + r * classes
+            hit = jnp.where(label == kind.astype(float_type), 1.0, 0.0).astype(low_type)
+            hot[128 * n : 128 * (n + 1), :] = jnp.concatenate([hit, hit, hit], axis=0).T
+        found = jnp.dot(hot[...], three_terms(back), preferred_element_type=float_type)
+        gc_ref[...] += found[0:classes]
+        return 0
 
     def vec(n):
         return vec_ref[n : n + 1, :]
@@ -705,7 +1011,8 @@
 
     for b in range(images):
         act_t[:, b * span + pixels : (b + 1) * span] = jnp.zeros((channels, 2 * width), low_type)
-    pl.semaphore_wait(barrier, 3)
+    pl.semaphore_wait(barrier, len(greeted))
+    red0.core()
 
     def step0(b, _):
         u = ag_ref[b]
@@ -717,6 +1024,7 @@
         return 0
 
     lax.fori_loop(0, images, step0, 0)
+    red0.across_x()
 
     def step1(b, _):
         first, second = receive_stats(0, b)
@@ -747,8 +1055,8 @@
         v = upstream * slope_of(pre)
         slope_grad[b] = v
         first, second = col_sum(v), col_sum(v * normed)
-        mg_ref[b, 0:1] = vec(3) * second + vec(4) * first
-        mg_ref[b, 1:2] = first
+        mg_ref[pl.ds(b, 1), 0:channels] = vec(3) * second + vec(4) * first
+        mg_ref[pl.ds(b, 1), channels:] = first
         first, second = grow * first, grow * second
         gs_ref[3:4] += second
         gs_ref[4:5] += first
@@ -756,7 +1064,18 @@
         return 0
 
     lax.fori_loop(0, images, step2, 0)
-    kernel_grad(act2_ref, grad2, gw2_ref)
+    red0.across_y()
+    kernel_grad(act2_ref, grad2, 0)
+    for n in range(3):
+        red2[n].core()
+    gs_ref[8:11] = sums_ref[0:3]
+    small_row(0)
+    gather_row()
+    for n in range(3):
+        red2[n].across_x()
+    red0.across_z()
+    small_y(0)
+    gather_y()
 
     def step3(b, _):
         first, second = receive_stats(2, b)
@@ -782,7 +1101,15 @@
         return 0
 
     lax.fori_loop(0, images, step4, 0)
-    kernel_grad(act1_ref, grad1, gw1_ref)
+    kernel_grad(act1_ref, grad1, 3)
+    for n in range(3):
+        red1[n].core()
+    small_z(0)
+    gather_z()
+    red0.back_z()
+    red2[0].across_y()
+    for n in range(3):
+        red1[n].across_x()
 
     def step5(b, _):
         upstream = data_grad(grad1, b, w1)
@@ -796,6 +1123,10 @@
         return 0
 
     lax.fori_loop(0, images, step5, 0)
+    small_row(1)
+    red0.back_y()
+    red2[1].across_y()
+    red2[0].across_z()
 
     def step6(b, _):
         first, second = receive_stats(4, b)
@@ -811,11 +1142,59 @@
         return 0
 
     lax.fori_loop(0, images, step6, 0)
-
-
-def backward_call(ag, mid, cot, hid, x, act1, act2, stats, vectors, modulate, w1, w2):
+    small_y(1)
+    small_end(0)
+    gather_end()
+    loads[2].wait()
+    embedding()
+    red0.end()
+    red2[2].across_y()
+    red2[1].across_z()
+    red2[0].back_z()
+    small_z(1)
+    red1[0].across_y()
+    red2[2].across_z()
+    red2[1].back_z()
+    red2[0].back_y()
+    red1[1].across_y()
+    red1[0].across_z()
+    red2[2].back_z()
+    red2[1].back_y()
+    red2[0].end()
+    red1[2].across_y()
+    red1[1].across_z()
+    red1[0].back_z()
+    red2[2].back_y()
+    red2[1].end()
+    red1[2].across_z()
+    red1[1].back_z()
+    red1[0].back_y()
+    red2[2].end()
+    red1[2].back_z()
+    red1[1].back_y()
+    red1[0].end()
+    red1[2].back_y()
+    red1[1].end()
+    red1[2].end()
+    small_end(1)
+    for red in [red0] + red1 + red2:
+        red.drain()
+    for s in range(2):
+        for cp in small_row_copies(s) + small_y_copies(s) + small_z_copies(s) + small_e_copies(s):
+            cp.wait_send()
+    for cp in gather_row_copies() + gather_copies():
+        cp.wait_send()
+
+
+def backward_call(
+    ag, mid, cot, hid, x, act1, act2, stats, vectors, modulate, joint, sums, emb, w1, w2, ew, classes
+):
     images, pixels, channels = x.shape
     span = pixels + 64
+    padded = -(-9 * channels // 4 // 128) * 128
+    every = lax.axis_size("img")
+    more = every // 8
+    some = max(more - 1, 1)
     vm = pl.BlockSpec(memory_space=pltpu.VMEM)
     hbm = pl.BlockSpec(memory_space=pl.ANY)
 
@@ -829,27 +1208,50 @@
         backward_kernel,
         out_shape=(
             jax.ShapeDtypeStruct(x.shape, float_type),
-            jax.ShapeDtypeStruct(w1.shape, low_type),
-            jax.ShapeDtypeStruct(w2.shape, low_type),
-            jax.ShapeDtypeStruct((images, 8, channels), float_type),
-            jax.ShapeDtypeStruct((16, channels), float_type),
+            jax.ShapeDtypeStruct((padded, channels), low_type),
+            jax.ShapeDtypeStruct((padded, channels), low_type),
+            jax.ShapeDtypeStruct((channels, channels), low_type),
+            jax.ShapeDtypeStruct((2, 16, channels), float_type),
+            jax.ShapeDtypeStruct((2 * channels // 4, 2 * channels), float_type),
+            jax.ShapeDtypeStruct((classes // 4, 2 * channels), float_type),
+            jax.ShapeDtypeStruct((8, 2 * channels), float_type),
         ),
-        in_specs=[vm] * 10 + [hbm] * 2,
-        out_specs=(vm,) * 5,
+        in_specs=[vm] * 13 + [hbm] * 3,
+        out_specs=(vm,) * 8,
         scratch_shapes=[
-            low(*w1.shape), low(*w2.shape), low(channels, channels),
+            low(*w1.shape), low(*w2.shape), low(*ew.shape), low(channels, channels),
             low(images, span, 3 * channels), low(images, span, 3 * channels),
             low(channels, images * span), wide(images, pixels, channels),
             wide(images, pixels, channels), low(5, images, 48, channels),
             low(5, images, 48, channels), low(5, images, 3, 48, channels),
-            pltpu.SemaphoreType.DMA((2,)), pltpu.SemaphoreType.DMA((5, images, 6)),
-            pltpu.SemaphoreType.DMA((5, images, 6)),
+            wide(16, channels), wide(8, 2 * channels),
+            low(6, 4, padded, 128), low(6, 2, padded, 128), low(6, padded, 128),
+            low(6, padded, 128), wide(6, padded, 128), low(6, padded // 2, 128),
+            low(6, padded // 2, 128), low(6, padded // 2, 128), low(6, 3, padded // 8, 128),
+            low(6, some, padded // 8, 128),
+            low(2, channels, channels), low(channels, channels), low(channels, channels),
+            wide(channels, channels), low(channels // 2, channels), low(channels // 2, channels),
+            low(channels // 2, channels), low(3, channels // 8, channels),
+            low(some, channels // 8, channels),
+            wide(2, 16, channels), wide(2, 3, 16, channels), wide(2, 16, channels),
+            wide(2, 16, channels),
+            wide(2, 16, channels), wide(2, 3, 16, channels), wide(2, 16, channels),
+            wide(2, some, 16, channels), wide(3, 8, 2 * channels), wide(every, 8, 2 * channels),
+            low(2 * channels, 192), low(256, 192),
+            pltpu.SemaphoreType.DMA((3,)), pltpu.SemaphoreType.DMA((5, images, 6)),
+            pltpu.SemaphoreType.DMA((5, images, 6)), pltpu.SemaphoreType.DMA((7, 11)),
+            pltpu.SemaphoreType.DMA((7, 11)), pltpu.SemaphoreType.DMA((7, some)),
+            pltpu.SemaphoreType.DMA((7, some)), pltpu.SemaphoreType.DMA((2, 6 + more)),
+            pltpu.SemaphoreType.DMA((2, 6 + more)), pltpu.SemaphoreType.DMA((6 + more,)),
+            pltpu.SemaphoreType.DMA((6 + more,)),
         ],
         compiler_params=pltpu.CompilerParams(
             collective_id=2, has_side_effects=True, vmem_limit_bytes=56 << 20
         ),
         name="backward",
-    )(ag, mid, cot, hid, x, act1, act2, stats, vectors, modulate, w1, w2)
+    )(
+        ag, mid, cot, hid, x, act1, act2, stats, vectors, modulate, joint, sums, emb, w1, w2, ew
+    )
 
 
 def shards(
@@ -909,77 +1311,38 @@
         [joint_offset[:channels], joint_offset[channels:], output_offset]
     ).astype(float_type)
     cot = cotangent.reshape(image_count, pixels, channels)
-    result, attend_grad, joint_weight_grad, output_weight_grad, sums = attention_call(
+    result, attend_grad, joint_blocks, offset_sums = attention_call(
         attend, middle, cot, attention_vectors, joint_weight, output_weight
     )
-    result = result.reshape(layout)
-    joint_offset_grad = jnp.concatenate([sums[0], sums[1]])
-    output_offset_grad = sums[2]
-    images_gradient, first_kernel_grad, second_kernel_grad, modulate_grad, sums = backward_call(
+    marks = jnp.repeat(labels.astype(float_type), 2 * channels // image_count)[None]
+    rows = jnp.concatenate([jnp.zeros_like(embedded), embedded, marks, jnp.zeros_like(marks)])
+    (
+        images_gradient, first_block, second_block, joint_block, sums, embed_weight_grad,
+        class_table_grad, embed_offset_grad,
+    ) = backward_call(
         attend_grad, middle, cot, hidden, x, act_one, act_two, stats, vectors,
-        modulate.reshape(image_count, 2, channels), first_kernel, second_kernel,
+        modulate.reshape(image_count, 2, channels), joint_blocks, offset_sums, rows,
+        first_kernel, second_kernel, embed_weight, class_count,
     )
-    images_gradient = images_gradient.reshape(layout)
-    (
-        first_gain_grad, first_shift_grad, first_offset_grad, second_gain_grad, second_shift_grad,
-        second_offset_grad, third_gain_grad, third_shift_grad,
-    ) = (sums[n] for n in range(8))
-    modulate_grad = modulate_grad[:, :2].reshape(image_count, 2 * channels)
-    modulate_grad = lax.psum(modulate_grad, "row")
-    every_grad, every_embedded, every_label = lax.all_gather(
-        (modulate_grad, embedded, labels), "img", axis=0, tiled=True
+    stripe = lax.axis_index("row")
+    size = channels // 4
+    own = lax.dynamic_slice_in_dim(sums, stripe * size, size, 2)
+    both = lax.dynamic_slice_in_dim(
+        jnp.concatenate([sums[0, 8], sums[0, 9]]), stripe * 2 * size, 2 * size, 0
     )
-    stripe_index = lax.axis_index("row")
-    stripe_count = lax.axis_size("row")
-
-    def own_rows(v, axis):
-        size = v.shape[axis] // stripe_count
-        return lax.dynamic_slice_in_dim(v, stripe_index * size, size, axis)
-
-    every_act = jax.nn.silu(every_embedded).astype(low_type).astype(float_type)
-    embed_weight_grad = lax.dot_general(
-        own_rows(every_act, 1), every_grad, contract_rows, precision=highest
+    embed_offset_grad = lax.dynamic_slice_in_dim(
+        embed_offset_grad[0], stripe * 2 * size, 2 * size, 0
     )
-    embed_offset_grad = own_rows(jnp.sum(every_grad, axis=0), 0)
-    active_grad = lax.dot_general(
-        every_grad, embed_weight.astype(float_type), contract_cols, precision=highest
-    )
-    embedded_grad = active_grad * silu_slope(every_embedded)
-    own_classes = stripe_index * (class_count // stripe_count) + jnp.arange(
-        class_count // stripe_count, dtype=jnp.int32
-    )
-    own_hot = (every_label[:, None] == own_classes[None, :]).astype(float_type)
-    class_table_grad = lax.dot_general(own_hot, embedded_grad, contract_rows, precision=highest)
-
-    def scattered(v):
-        v = lax.psum_scatter(v.astype(low_type), "row", scatter_dimension=0, tiled=True)
-        return lax.psum(v.astype(low_type), "img").astype(float_type)
-
-    first_kernel_grad, second_kernel_grad, joint_weight_grad, output_weight_grad = (
-        scattered(v)
-        for v in (first_kernel_grad, second_kernel_grad, joint_weight_grad, output_weight_grad)
-    )
-    small = (
-        first_gain_grad, first_shift_grad, first_offset_grad, second_gain_grad, second_shift_grad,
-        second_offset_grad, third_gain_grad, third_shift_grad, joint_offset_grad,
-        output_offset_grad,
-    )
-    summed = lax.psum(jnp.concatenate(small), ("img", "row"))
-    pieces, at = [], 0
-    for v in small:
-        pieces.append(own_rows(summed[at : at + v.shape[0]], 0))
-        at += v.shape[0]
-    (
-        first_gain_grad, first_shift_grad, first_offset_grad, second_gain_grad, second_shift_grad,
-        second_offset_grad, third_gain_grad, third_shift_grad, joint_offset_grad,
-        output_offset_grad,
-    ) = pieces
+    quarter = 9 * channels // 4
+    joint_weight_grad = jnp.concatenate(
+        [joint_block[n * size : (n + 1) * size] for n in range(3)], axis=1
+    ).astype(float_type)
     return (
-        result, images_gradient, first_gain_grad, first_shift_grad, first_kernel_grad,
-        first_offset_grad, embed_weight_grad, embed_offset_grad, class_table_grad,
-        second_gain_grad, second_shift_grad, second_kernel_grad, second_offset_grad,
-        third_gain_grad, third_shift_grad, joint_weight_grad, joint_offset_grad,
-        output_weight_grad, output_offset_grad,
+        result.reshape(layout), images_gradient.reshape(layout), own[1, 0], own[1, 1],
+        first_block[:quarter].astype(float_type), own[1, 2], embed_weight_grad,
+        embed_offset_grad, class_table_grad, own[0, 3], own[0, 4],
+        second_block[:quarter].astype(float_type), own[0, 5], own[0, 6], own[0, 7],
+        joint_weight_grad, both, joint_block[3 * size :].astype(float_type), own[0, 10],
     )
 
 

time: 366 us -> 213 us (0.58)
  blocking collectives: 122 us -> 0 us
  waiting for transfers between devices: 81.7 us -> 0 us
  Pallas kernels: 110 us -> 187 us
  between operations: 14.7 us -> 0.83 us
  other arithmetic: 12.8 us -> 8.23 us
  local copies, waits for them, and re-layouts: 18.9 us -> 14.9 us
  matrix products: 5.15 us -> 1.28 us
    reduce_scatter x4 -> x0, waiting for transfers between devices: 81.2 us -> none  [scattered(): lax.psum_scatter(v.astype(low_type), 'row', scatter_dimension=0, tiled=True)]
    pallas_call x1, Pallas kernels: 36.1 us -> 113 us  [backward_call(): pl.pallas_call(backward_kernel, out_shape=(jax.ShapeDtypeStruct(x.shape,...]
    all_gather x2 -> x0, blocking collectives: 61.7 us -> none  [shards(): lax.all_gather((modulate_grad, embedded, labels), 'img', axis=0, tiled=True)]
    psum x2 -> x0, blocking collectives: 48.6 us -> none  [the longest x1 37.6 us: shards(): summed = lax.psum(jnp.concatenate(small), ('img', 'row'))]
    unnamed x1 -> x0, blocking collectives: 11.5 us -> none
    dynamic_slice x11 -> x2, local copies, waits for them, and re-layouts: 6.52 us -> 1.28 us  [the longest x1 0.64 us: shards(): lax.dynamic_slice_in_dim(jnp.concatenate([sums[0, 8], sums[0, 9]]), strip...]
    convert_element_type x6 -> x4, other arithmetic: 10 us -> 5.5 us  [the longest x1 3.02 us: shards(): second_block[:quarter].astype(float_type)]
    dot_general x3 -> x0, matrix products: 3.87 us -> none  [the longest x1 1.47 us: shards(): lax.dot_general(own_hot, embedded_grad, contract_rows, precision=highest)]
  transfers between devices with their start and end apart: 5 -> 0, of which waited for: 3 -> 0; matrix products, arithmetic and copies ran while one was open for 4% -> 0% of each run, Pallas kernels for 10% -> 0%
where the time goes in v1:
time: 213 us; the launch traced here: 212 us
  Pallas kernels  187 us (88%)
  local copies, waits for them, and re-layouts  14.9 us (7%)
  other arithmetic  8.23 us (4%)
    pallas_call x1, Pallas kernels, backward_call(): pl.pallas_call(backward_kernel, out_shape=(jax.ShapeDtypeStruct(x.shape,...  113 us
    pallas_call x1, Pallas kernels, attention_call(): pl.pallas_call(attention_kernel, out_shape=(jax.ShapeDtypeStruct(att.shap...  51.9 us
    pallas_call x1, Pallas kernels, forward_call(): pl.pallas_call(forward_kernel, out_shape=(wide, wide, low, low, low, jax....  21.9 us
    another operation x9, local copies, waits for them, and re-layouts, shards(): jnp.stack([first_gain, first_shift, first_offset, second_gain, second_shi...  5.65 us

profile of v1, /device:TPU:0, one launch (start us, length us, event | category | flops | bytes accessed | tf_op | source)
XLA Modules:
  0.0 212.1 jit_solution(13062081803903717903)
XLA Ops:
  0.7 0.8 stack.39
  1.5 0.7 stack.40
  2.2 0.7 stack.41
  2.9 0.7 stack.42
  3.6 0.7 stack.43
  4.3 0.7 stack.44
  4.9 0.7 stack.45
  5.6 0.7 stack.46
  6.3 0.6 convert_element_type.34.vec_ref
  7.0 0.7 log_multiply_fusion
  7.6 0.1 multiply_cosine_fusion
  7.8 1.0 convolution_add_fusion
  8.8 0.3 convolution_add_fusion.1
  9.1 0.6 reshape.64.mod_ref
  9.7 21.9 %forward.1 = (f32[3,256,384]{2,1,0:T(8,128)}, f32[3,256,384]{2,1,0:T(8,128)}, bf16[3,256,384]{2,1,0:T(8,128)(2,1)}, bf16[3,256,384]{2,1,0:T(8,128)(2,1)}, bf16[3...) custom-call(bf16[3,256,384]{2,1,0:T(8,128)(2,1)} %bitcast.30, f32[8,384]{1,0:T(8,128)} %convert_element_type.34.vec_ref, ...), custom_call_target="tpu_custom_call" | custom-call | tf_op jit(solution)/shard_map/forward/pallas_call | solution.py:308
  31.8 0.6 maximum_convert_fusion.1.vec_ref
  32.4 51.9 %attention.1 = (bf16[3,256,384]{2,1,0:T(8,128)(2,1)}, f32[3,256,384]{2,1,0:T(8,128)}, bf16[4,384,384]{2,1,0:T(8,128)(2,1)}, f32[8,384]{1,0:T(8,128)}) custom-call(bf16[3,256,384]{2,1,0:T(8,128)(2,1)} %get-tuple-element.37.att_ref, f32[3,256,384]{2,1,0:T(8,128)} %get-tuple-element.38.mid_ref, bf16[3,256,384]{2,1,0:T(8,128)(2,1)} %bitcast.32, ...), custom_call_target="tpu_custom_call" | custom-call | tf_op jit(solution)/shard_map/attention/pallas_call | solution.py:563
  84.5 0.7 maximum_maximum_fusion.emb_ref
  85.2 113.0 %backward.1 = (f32[3,256,384]{2,1,0:T(8,128)}, bf16[896,384]{1,0:T(8,128)(2,1)}, bf16[896,384]{1,0:T(8,128)(2,1)}, bf16[384,384]{1,0:T(8,128)(2,1)}, f32[2,16,38...) custom-call(f32[3,256,384]{2,1,0:T(8,128)} %get-tuple-element.40.ag_ref, ...), custom_call_target="tpu_custom_call" | custom-call | tf_op jit(solution)/shard_map/backward/pallas_call | solution.py:1207
  198.2 1.5 fusion.4
  199.7 3.0 %slice_convert_fusion = (f32[864,384]{1,0:T(8,128)}, f32[864,384]{1,0:T(8,128)}) fusion(bf16[896,384]{1,0:T(8,128)(2,1)} %get-tuple-element.53, bf16[896,384]{1,0:T(8,128)(2,1)} %get-tuple-element.49), kind=kLoop, calls=%fused_computation.2 | loop fusion | flops 663552 | bytes 3981312 | tf_op jit(solution)/shard_map/convert_element_type | solution.py:1344
  202.7 0.8 slice.66
  203.6 0.6 constant_dynamic-slice_fusion.6
  204.2 1.7 slice_convert_fusion.2
  205.9 0.8 maximum_convert_fusion
  206.7 0.8 slice_reduce_fusion.1
  207.5 0.6 dynamic_slice.14
  208.1 0.8 copy.46
  209.0 1.0 copy.47
  210.0 0.4 copy-done.5
  210.4 0.8 copy.48
  211.2 0.9 copy.49
  (33 shorter events, 0.3 us)
Async XLA Ops:
  0.7 7.1 %copy-start = (bf16[1000,768]{1,0:T(8,128)(2,1)S(1)}, bf16[1000,768]{1,0:T(8,128)(2,1)}, u32[]{:S(2)}) copy-start(bf16[1000,768]{1,0:T(8,128)(2,1)} %param.32) | copy-start | bytes 4608004
  0.7 8.1 %copy-start.1 = (bf16[768,768]{1,0:T(8,128)(2,1)S(1)}, bf16[768,768]{1,0:T(8,128)(2,1)}, u32[]{:S(2)}) copy-start(bf16[768,768]{1,0:T(8,128)(2,1)} %ew_any.1) | copy-start | bytes 3538948
  0.7 8.1 %copy-start.6 = (bf16[768]{0:T(1024)(128)(2,1)S(1)}, bf16[768]{0:T(1024)(128)(2,1)}, u32[]{:S(2)}) copy-start(bf16[768]{0:T(1024)(128)(2,1)} %param.31) | copy-start | bytes 4612
  9.7 22.0 %copy-start.8 = (bf16[384]{0:T(512)(128)(2,1)S(1)}, bf16[384]{0:T(512)(128)(2,1)}, u32[]{:S(2)}) copy-start(bf16[384]{0:T(512)(128)(2,1)} %param.42) | copy-start | bytes 2308
  9.7 22.0 %copy-start.7 = (bf16[768]{0:T(1024)(128)(2,1)S(1)}, bf16[768]{0:T(1024)(128)(2,1)}, u32[]{:S(2)}) copy-start(bf16[768]{0:T(1024)(128)(2,1)} %param.40) | copy-start | bytes 4612
  32.4 51.9 %copy-start.9 = (s32[3]{0:T(128)S(1)}, s32[3]{0:T(128)}, u32[]{:S(2)}) copy-start(s32[3]{0:T(128)} %param.25) | copy-start | bytes 40
  199.7 8.4 %copy-start.4 = (bf16[3,256,384]{2,1,0:T(8,128)(2,1)S(1)}, bf16[3,256,384]{2,1,0:T(8,128)(2,1)}, u32[]{:S(2)}) copy-start(bf16[3,256,384]{2,1,0:T(8,128)(2,1)} %get-tuple-element.39) | copy-start | bytes 1769476
  202.7 6.2 %copy-start.2 = (f32[3,256,384]{2,1,0:T(8,128)S(1)}, f32[3,256,384]{2,1,0:T(8,128)}, u32[]{:S(2)}) copy-start(f32[3,256,384]{2,1,0:T(8,128)} %get-tuple-element.47) | copy-start | bytes 3538948
  209.0 1.4 copy-start.5
  209.0 2.3 %copy-start.3 = (f32[250,768]{1,0:T(8,128)S(1)}, f32[250,768]{1,0:T(8,128)}, u32[]{:S(2)}) copy-start(f32[250,768]{1,0:T(8,128)} %get-tuple-element.103) | copy-start | bytes 2304004
